TPU v7x, 256 devices: a whole 4x4x8 slice. The times are simulated.
256 devices in a mesh: cohort: 4 (over y), gene: 64 (over x, z, core).
Axes of the slice: x: 4, y: 4, z: 8, core: 2. Of those that a mesh axis runs over, the one named last changes fastest.
Arguments:
- scores: bfloat16 [4, 393216, 512], P('cohort', 'gene'), may hold values from -6 to 6
- flips: int32 [4, 393216], P('cohort', 'gene'), may hold values from 0 to 1
- presence: int32 [4, 393216], P('cohort', 'gene'), may hold values 0 or 1
- covs: bfloat16 [4, 3072, 128, 128], P('cohort', 'gene'), may hold values from -2 to 2.5, as said below
- membership: int32 [8, 393216], P(None, 'gene'), may hold values 0 or 1
- weights: float32 [393216], P('gene'), may hold values from 0.25 to 4
- tile_owner: int32 [3072, 1], P('gene'), may hold values from 0 to 63; in each aligned block of 48 rows (0 to 47, 48 to 95, ...) at most 2 rows name the same one
- tile_gene: int32 [3072], P('gene'), may hold values from 0 to 15
Outputs:
- burden_z: float32 [1024, 8, 512], P('gene', None, 'cohort')
- skat_z: float32 [1024, 8, 512], P('gene', None, 'cohort')
Inputs may be any that keep to these rules, and one draw needn't show every extreme that they name: `tile_owner`: in the tiles of one device (aligned blocks of 48 tiles) at most 2 belong to one owner. `covs`: each block is symmetric.
All inputs are finite; a program needn't handle non-finite values. No bound on the sum of `presence` or of `membership` on one device may be relied on, other than what follows from the above.
Results may differ from a plain program's by a relative error of at most 0.035.
Values may be sent and summed in bfloat16 or wider, within the bound.
A program may use at most 128 MiB of HBM per device.

v0:
```python
import jax
import jax.numpy as jnp
from jax import lax
from jax.sharding import PartitionSpec as P

GENE_DEV = 16


def score_stats(u_rows, w_rows):
    tile_burden = jnp.einsum("kmv,kvp->kmp", w_rows, u_rows, preferred_element_type=jnp.float32)
    w_wide = w_rows.astype(jnp.float32)
    u_wide = u_rows.astype(jnp.float32)
    tile_square = jnp.einsum(
        "kmv,kvp->kmp", w_wide * w_wide, u_wide * u_wide, precision=lax.Precision.HIGHEST
    )
    return (tile_burden, tile_square)


def block_moments(v_rows, w_rows):
    w_wide = w_rows.astype(jnp.float32)
    w_square = w_wide * w_wide
    carried = jnp.einsum("kij,kmj->kmi", v_rows, w_rows, preferred_element_type=jnp.float32)
    tile_variance = jnp.sum(carried * w_wide, axis=2)
    v_wide = v_rows.astype(jnp.float32)
    diagonal = jnp.diagonal(v_wide, axis1=1, axis2=2)
    tile_trace = jnp.sum(w_square * diagonal[:, None, :], axis=2)
    squared = jnp.einsum("kij,kmj->kmi", v_wide * v_wide, w_square, precision=lax.Precision.HIGHEST)
    tile_spread = jnp.sum(squared * w_square, axis=2)
    return (tile_variance, tile_trace, tile_spread)


def flatten_slots(value):
    return value.reshape((-1,) + value.shape[2:])


def shards(scores, flips, presence, covs, membership, weights, tile_owner, tile_gene):
    owner_count = lax.axis_size("gene")
    tile_count = tile_gene.shape[0]
    tile_width = covs.shape[-1]
    mask_count = membership.shape[0]
    allele_sign = 1.0 - 2.0 * flips[0].astype(jnp.float32)
    factor = allele_sign * presence[0].astype(jnp.float32)
    signed = scores[0].astype(jnp.float32) * factor[:, None]
    united = lax.psum_scatter(
        signed.astype(jnp.bfloat16), "cohort", scatter_dimension=1, tiled=True
    )
    united = lax.optimization_barrier(united)
    u_rows = united.reshape(tile_count, tile_width, united.shape[1])
    mask_weights = (weights[None, :] * (1.0 + 3.0 * membership.astype(jnp.float32)) / 4.0).astype(
        jnp.bfloat16
    )
    w_rows = jnp.transpose(mask_weights.reshape(mask_count, tile_count, tile_width), (1, 0, 2))
    tile_sign = allele_sign.reshape(tile_count, tile_width)
    cov_term = covs[0].astype(jnp.float32) * tile_sign[:, :, None] * tile_sign[:, None, :]
    slot_count = max(2, (2 * tile_count + owner_count - 1) // owner_count)
    owners = tile_owner[:, 0]
    ordinal = jnp.arange(tile_count, dtype=jnp.int32)
    matched = owners[:, None] == owners[None, :]
    earlier = ordinal[:, None] > ordinal[None, :]
    ordinal_rank = jnp.sum((matched & earlier).astype(jnp.int32), axis=1)
    slot_index = owners * slot_count + ordinal_rank
    slot_ids = jnp.arange(owner_count * slot_count, dtype=jnp.int32)
    chosen = (slot_index[None, :] == slot_ids[:, None]).astype(jnp.int32)
    source = jnp.sum(chosen * ordinal[None, :], axis=1)
    filled = jnp.sum(chosen, axis=1) > 0

    def packed_slots(payload):
        taken = jnp.take(payload, source, axis=0)
        keep = filled.reshape((-1,) + (1,) * (payload.ndim - 1))
        taken = jnp.where(keep, taken, jnp.zeros_like(taken))
        return taken.reshape((owner_count, slot_count) + payload.shape[1:])

    gene_slots = jnp.where(filled, jnp.take(tile_gene, source, axis=0), -1).reshape(
        owner_count, slot_count
    )
    blocks = lax.psum(cov_term.astype(jnp.bfloat16), "cohort")
    u_got = lax.all_to_all(packed_slots(u_rows), "gene", split_axis=0, concat_axis=0, tiled=True)
    v_got = lax.all_to_all(packed_slots(blocks), "gene", split_axis=0, concat_axis=0, tiled=True)
    w_got = lax.all_to_all(packed_slots(w_rows), "gene", split_axis=0, concat_axis=0, tiled=True)
    g_got = lax.all_to_all(
        gene_slots.astype(jnp.bfloat16), "gene", split_axis=0, concat_axis=0, tiled=True
    )
    leading = u_got.shape[:2]
    w_flat = flatten_slots(w_got)
    tile_burden, tile_square = score_stats(flatten_slots(u_got), w_flat)
    tile_variance, tile_trace, tile_spread = block_moments(flatten_slots(v_got), w_flat)
    received = (
        tile_burden.reshape(leading + tile_burden.shape[1:]),
        tile_square.reshape(leading + tile_square.shape[1:]),
        tile_variance.reshape(leading + tile_variance.shape[1:]),
        tile_trace.reshape(leading + tile_trace.shape[1:]),
        tile_spread.reshape(leading + tile_spread.shape[1:]),
        g_got,
    )
    got_burden, got_square, got_variance, got_trace, got_spread, got_genes = received
    gene_flat = got_genes.reshape(-1).astype(jnp.int32)
    onehot = (gene_flat[:, None] == jnp.arange(GENE_DEV, dtype=jnp.int32)[None, :]).astype(
        jnp.float32
    )
    gene_burden = jnp.einsum(
        "sg,smp->gmp", onehot, flatten_slots(got_burden), precision=lax.Precision.HIGHEST
    )
    gene_square = jnp.einsum(
        "sg,smp->gmp", onehot, flatten_slots(got_square), precision=lax.Precision.HIGHEST
    )
    gene_variance = jnp.einsum(
        "sg,sm->gm", onehot, flatten_slots(got_variance), precision=lax.Precision.HIGHEST
    )
    gene_trace = jnp.einsum(
        "sg,sm->gm", onehot, flatten_slots(got_trace), precision=lax.Precision.HIGHEST
    )
    gene_spread = jnp.einsum(
        "sg,sm->gm", onehot, flatten_slots(got_spread), precision=lax.Precision.HIGHEST
    )
    burden_z = gene_burden / jnp.sqrt(jnp.maximum(gene_variance, 1.0))[:, :, None]
    skat_z = (gene_square - gene_trace[:, :, None]) / jnp.sqrt(jnp.maximum(2.0 * gene_spread, 1.0))[
        :, :, None
    ]
    return (burden_z, skat_z)


def solution(mesh):
    return jax.shard_map(
        shards,
        mesh=mesh,
        in_specs=(
            P("cohort", "gene", None),
            P("cohort", "gene"),
            P("cohort", "gene"),
            P("cohort", "gene", None, None),
            P(None, "gene"),
            P("gene"),
            P("gene", None),
            P("gene"),
        ),
        out_specs=(P("gene", None, "cohort"), P("gene", None, "cohort")),
        check_vma=False,
    )
```

profile of v0, /device:TPU:1, one launch (start us, length us, event | category | flops | bytes accessed | tf_op | source)
XLA Modules:
  0.0 430.9 jit_solution(12299920613399019426)
XLA Ops:
  7.2 0.8 multiply_subtract_fusion
  8.0 3.0 fusion.5
  11.1 7.0 %fusion = bf16[6144,512]{1,0:T(8,128)(2,1)} fusion(bf16[1,6144,512]{2,1,0:T(8,128)(2,1)} %param.10, f32[6144]{0:T(1024)S(1)} %bitcast.60), kind=kLoop, calls=%fused_computation.6 | loop fusion | flops 9437184 | bytes 12607488 | tf_op jit(solution)/shard_map/convert_element_type | solution.py:45
  18.1 8.7 %copy.47 = bf16[6144,512]{0,1:T(8,128)(2,1)} copy(bf16[6144,512]{1,0:T(8,128)(2,1)} %fusion) | data formatting | bytes 12582912
  26.8 0.6 copy-done.6
  27.4 0.2 convert_reduce_fusion.2
  27.6 0.1 convert_reduce_fusion.1
  27.7 0.1 reduce_sum.65
  27.9 0.1 gt.49
  28.2 1.2 gather_fusion
  29.4 0.1 gather.20
  29.7 0.7 copy.39
  30.4 13.0 %all-to-all-start = ((bf16[64,1,2]{2,1,0:T(2,128)(2,1)}), bf16[64,1,2]{2,1,0:T(2,128)(2,1)S(1)}, u32[]{:S(2)}, u32[]{:S(2)}) async-start(bf16[64,1,2]{2,1,0:T(2,128)(2,1)} %copy.39), calls=%async_computation | async-start | bytes 65536 | tf_op jit(solution)/shard_map/all_to_all | solution.py:80
  43.4 0.1 reduce_sum.67
  43.6 0.2 gt.52
  43.8 0.7 gather_fusion.1
  44.5 1.0 select_select_fusion.2
  45.6 24.9 %all-reduce.2.cloned.1.call-done = bf16[48,128,128]{2,1,0:T(8,128)(2,1)} async-done(((bf16[48,128,128]{2,1,0:T(8,128)(2,1)}), bf16[48,128,128]{2,1,0:T(8,128)(2,1)}) %all-reduce.2.cloned.1.call-update) | async-done | bytes 1572880 | tf_op jit(solution)/shard_map/psum | solution.py:76
  70.5 4.5 %gather_fusion.4 = bf16[128,128,128]{2,1,0:T(8,128)(2,1)} fusion(bf16[48,128,128]{2,1,0:T(8,128)(2,1)} %all-reduce.2.cloned.1.call-done, s32[1024]{0:T(1024)S(1)} %pad_clamp_fusion), kind=kCustom, calls=%fused_computation.1.clone | custom fusion | bytes 8389120 | tf_op jit(solution)/shard_map/jit(_take)/gather | solution.py:68
  75.0 64.8 %reduce-scatter.4.cloned.1.call-done = bf16[128,6144]{1,0:T(8,128)(2,1)} async-done(((bf16[512,6144]{1,0:T(8,128)(2,1)}), bf16[128,6144]{1,0:T(8,128)(2,1)}) %reduce-scatter.4.cloned.1.call-update) | async-done | bytes 1572880
  139.9 1.9 copy.48
  141.8 3.2 gather_fusion.3
  145.0 10.6 %all-to-all-start.1 = ((bf16[64,2,8,128]{3,2,1,0:T(8,128)(2,1)}), bf16[64,2,8,128]{3,2,1,0:T(8,128)(2,1)S(1)}, u32[]{:S(2)}, u32[]{:S(2)}) async-start(bf16[64,2,8,128]{3,2,1,0:T(8,128)(2,1)} %select_select_fusion.2), calls=%async_computation.1 | async-start | bytes 524288 | tf_op jit(solution)/shard_map/all_to_all | solution.py:79
  155.6 6.3 %select_select_fusion = (bf16[128,128,128]{2,1,0:T(8,128)(2,1)}, bf16[128,128,128]{2,1,0:T(8,128)(2,1)}) fusion(bf16[128,128,128]{2,1,0:T(8,128)(2,1)} %gather_fusion.4, pred[128]{0:T(512)(128)(4,1)S(1)} %get-tuple-element.19, pred[128]{0:T(512)(128)(4,1)S(1)} %get-tuple-element.20, bf16[128,128,128]{2,1,0:T(8,128)(2,1)} %gather_fusion.3), kind=kLoop, calls=%fused_computation.10 | loop fusion | flops 8388608 | bytes 16777472 | tf_op jit(solution)/shard_map/jit(_where)/select_n | solution.py:70
  161.9 5.7 %all-to-all-done.1 = bf16[64,2,8,128]{3,2,1,0:T(8,128)(2,1)S(1)} async-done(((bf16[64,2,8,128]{3,2,1,0:T(8,128)(2,1)}), bf16[64,2,8,128]{3,2,1,0:T(8,128)(2,1)S(1)}, u32[]{:S(2)}, u32[]{:S(2)}) %all-to-all-start.1) | async-done | bytes 262176 | tf_op jit(solution)/shard_map/all_to_all | solution.py:79
  167.6 102.3 %all_to_all.21 = bf16[64,2,128,128]{3,2,1,0:T(8,128)(2,1)} all-to-all(bf16[64,2,128,128]{3,2,1,0:T(8,128)(2,1)} %bitcast.49), channel_id=1, replica_groups=mesh['cohort'=4,'gene'=64] {'gene'}, dimensions={0} | all-to-all | bytes 8388608 | tf_op jit(solution)/shard_map/all_to_all | solution.py:77
  269.9 6.0 %all-to-all-start.3 = ((bf16[64,2,128,128]{3,2,1,0:T(8,128)(2,1)}), bf16[64,2,128,128]{3,2,1,0:T(8,128)(2,1)}, u32[]{:S(2)}, u32[]{:S(2)}) async-start(bf16[64,2,128,128]{3,2,1,0:T(8,128)(2,1)} %bitcast.48), calls=%async_computation.3 | async-start | bytes 8388608 | tf_op jit(solution)/shard_map/all_to_all | solution.py:78
  275.9 0.1 convert_reduce_fusion
  276.1 0.1 reshape.210
  276.2 3.5 fusion.28
  279.7 6.9 %fusion.1 = f32[128,8,128]{2,1,0:T(8,128)S(1)} fusion(bf16[128,128,128]{2,1,0:T(8,128)(2,1)S(1)} %bitcast.45, bf16[128,8,128]{2,1,0:T(8,128)(2,1)S(1)} %bitcast.51), kind=kOutput, calls=%fused_computation.7 | convolution fusion | flops 205783040 | bytes 4980736 | tf_op jit(solution)/shard_map/kmv,kvp->kmp/dot_general | solution.py:13
  286.6 85.2 %all-to-all-done.3 = bf16[64,2,128,128]{3,2,1,0:T(8,128)(2,1)} async-done(((bf16[64,2,128,128]{3,2,1,0:T(8,128)(2,1)}), bf16[64,2,128,128]{3,2,1,0:T(8,128)(2,1)}, u32[]{:S(2)}, u32[]{:S(2)}) %all-to-all-start.3) | async-done | bytes 4194336 | tf_op jit(solution)/shard_map/all_to_all | solution.py:78
  371.8 4.5 %fusion.6 = f32[128,8]{1,0:T(8,128)S(1)} fusion(bf16[128,8,128]{2,1,0:T(8,128)(2,1)S(1)} %bitcast.52, bf16[128,128,128]{2,1,0:T(8,128)(2,1)} %bitcast.16), kind=kOutput, calls=%fused_computation.18 | convolution fusion | flops 33946624 | bytes 4460544 | tf_op jit(solution)/shard_map/kij,kmj->kmi/dot_general | solution.py:22
  376.3 6.9 %copy.42 = bf16[128,128,128]{0,2,1:T(8,128)(2,1)} copy(bf16[128,128,128]{2,1,0:T(8,128)(2,1)} %bitcast.16) | data formatting | bytes 8388608 | tf_op jit(solution)/shard_map/reshape | solution.py:33
  383.3 6.8 %convert_multiply_fusion.2 = f32[128,128,128]{0,2,1:T(8,128)} fusion(bf16[128,128,128]{0,2,1:T(8,128)(2,1)} %copy.42), kind=kLoop, calls=%fused_computation.15 | loop fusion | flops 4194304 | bytes 12582912 | tf_op jit(solution)/shard_map/mul | solution.py:27
  390.0 4.3 convert_element_type.107
  394.3 0.2 fusion.11
  394.5 0.4 convolution_divide_fusion
  394.8 0.7 copy.45
  395.5 9.3 %copy.44 = f32[128,128,128]{2,1,0:T(8,128)} copy(f32[128,128,128]{0,2,1:T(8,128)} %convert_multiply_fusion.2) | data formatting | bytes 16777216 | tf_op jit(solution)/shard_map/mul | solution.py:27
  404.8 15.7 %fusion.7 = f32[128,8]{1,0:T(8,128)S(1)} fusion(f32[128,128,128]{2,1,0:T(8,128)} %copy.44, bf16[128,8,128]{2,1,0:T(8,128)(2,1)S(1)} %bitcast.53), kind=kOutput, calls=%fused_computation.19 | convolution fusion | flops 201849856 | bytes 8654848 | tf_op jit(solution)/shard_map/kij,kmj->kmi/dot_general | solution.py:27
  420.5 0.2 fusion.10
  420.7 1.8 gather_fusion.2
  422.5 0.1 copy.43
  422.6 0.3 multiply_reduce_fusion
  422.9 0.2 fusion.16
  423.1 0.4 fusion.8
  423.4 0.7 copy.46
  (31 shorter events, 0.5 us)
Async XLA Ops:
  7.2 21.0 %copy-start = (s32[48]{0:T(128)S(1)}, s32[48]{0:T(128)}, u32[]{:S(2)}) copy-start(s32[48]{0:T(128)} %param.17) | copy-start | bytes 580
  7.2 63.3 %all-reduce.2.cloned.1.call-start = ((), (), s32[]{:S(2)}) async-start(), calls=%async_computation.5 | async-start | bytes 3145728 | tf_op jit(solution)/shard_map/psum | solution.py:76
  11.1 128.8 %reduce-scatter.4.cloned.1.call-start = ((), (), s32[]{:S(2)}) async-start(), calls=%async_computation.6 | async-start | bytes 7864320
  26.8 0.7 copy-start.6
  26.8 16.9 %copy-start.4 = (s32[8,6144]{1,0:T(8,128)S(1)}, s32[8,6144]{1,0:T(8,128)}, u32[]{:S(2)}) copy-start(s32[8,6144]{1,0:T(8,128)} %param.14) | copy-start | bytes 589828
  26.8 17.0 %copy-start.5 = (f32[6144]{0:T(1024)S(1)}, f32[6144]{0:T(1024)}, u32[]{:S(2)}) copy-start(f32[6144]{0:T(1024)} %param.15) | copy-start | bytes 73732
  30.4 114.5 %all-to-all-start = ((bf16[64,1,2]{2,1,0:T(2,128)(2,1)}), bf16[64,1,2]{2,1,0:T(2,128)(2,1)S(1)}, u32[]{:S(2)}, u32[]{:S(2)}) async-start(bf16[64,1,2]{2,1,0:T(2,128)(2,1)} %copy.39), calls=%async_computation | async-start | bytes 65536 | tf_op jit(solution)/shard_map/all_to_all | solution.py:80
  145.0 22.6 %all-to-all-start.1 = ((bf16[64,2,8,128]{3,2,1,0:T(8,128)(2,1)}), bf16[64,2,8,128]{3,2,1,0:T(8,128)(2,1)S(1)}, u32[]{:S(2)}, u32[]{:S(2)}) async-start(bf16[64,2,8,128]{3,2,1,0:T(8,128)(2,1)} %select_select_fusion.2), calls=%async_computation.1 | async-start | bytes 524288 | tf_op jit(solution)/shard_map/all_to_all | solution.py:79
  269.9 101.9 %all-to-all-start.3 = ((bf16[64,2,128,128]{3,2,1,0:T(8,128)(2,1)}), bf16[64,2,128,128]{3,2,1,0:T(8,128)(2,1)}, u32[]{:S(2)}, u32[]{:S(2)}) async-start(bf16[64,2,128,128]{3,2,1,0:T(8,128)(2,1)} %bitcast.48), calls=%async_computation.3 | async-start | bytes 8388608 | tf_op jit(solution)/shard_map/all_to_all | solution.py:78
  276.2 3.5 copy-start.3
  383.2 6.8 %copy-start.2 = (bf16[128,128,128]{0,2,1:T(8,128)(2,1)S(1)}, bf16[128,128,128]{0,2,1:T(8,128)(2,1)}, u32[]{:S(2)}) copy-start(bf16[128,128,128]{0,2,1:T(8,128)(2,1)} %copy.42) | copy-start | bytes 12582916
  395.5 28.6 %copy-start.1 = (s32[48]{0:T(128)S(1)}, s32[48]{0:T(128)}, u32[]{:S(2)}) copy-start(s32[48]{0:T(128)} %param.17) | copy-start | bytes 580
Sparse Core Ops, SparseCore 0:
  11.2 59.2 all-reduce.1
  73.1 66.7 reduce-scatter.3
where the time goes:
time: 432 us; the launch traced here: 431 us
  waiting for transfers between devices  181 us (42%)
  blocking collectives  102 us (24%)
  local copies, waits for them, and re-layouts  42.1 us (10%)
  matrix products  32 us (7%)
  other arithmetic  30 us (7%)
  starting transfers between devices  29.7 us (7%)
  between operations  14.3 us (3%)
    all_to_all x1, blocking collectives, shards(): lax.all_to_all(packed_slots(u_rows), 'gene', split_axis=0, concat_axis=0,...  102 us
    all_to_all x1, waiting for transfers between devices, shards(): lax.all_to_all(packed_slots(blocks), 'gene', split_axis=0, concat_axis=0,...  85.2 us
    unnamed x3, waiting for transfers between devices  64.9 us
    psum x1, waiting for transfers between devices, shards(): blocks = lax.psum(cov_term.astype(jnp.bfloat16), 'cohort')  24.9 us
    dot_general x1, matrix products, block_moments(): jnp.einsum('kij,kmj->kmi', v_wide * v_wide, w_square, precision=lax.Preci...  15.7 us
    all_to_all x1, starting transfers between devices, shards(): lax.all_to_all(gene_slots.astype(jnp.bfloat16), 'gene', split_axis=0, con...  13 us
    unnamed x18, local copies, waits for them, and re-layouts  12.6 us
    all_to_all x1, starting transfers between devices, shards(): lax.all_to_all(packed_slots(w_rows), 'gene', split_axis=0, concat_axis=0,...  10.6 us
  transfers between devices with their start and end apart: 5, of which 4 were waited for; matrix products, arithmetic and copies ran while one was open for 11% of the time, Pallas kernels for 0%

commit v1 on v0

v1 whole, which is shorter than its diff:
```python
import functools

import jax
import jax.numpy as jnp
from jax import lax
from jax.experimental import pallas as pl
from jax.experimental.pallas import tpu as pltpu
from jax.sharding import PartitionSpec as P

F32, BF16 = jnp.float32, jnp.bfloat16
MESH = pl.DeviceIdType.MESH
TILE = 128
TILES = 48
HALF = TILES // 2
CHUNKS = 4
CHUNK_TILES = HALF // CHUNKS
CHUNK_ROWS = CHUNK_TILES * TILE
COHORTS = 4
OWNERS = 64
GENES = 16
MASKS = 8
OWN_TILES = TILES // COHORTS
PAIRS = OWN_TILES // 2
COV_ROWS = PAIRS // 2 * TILE + 16
HIGHEST = lax.Precision.HIGHEST


def rows_of(tile):
    return pl.ds(pl.multiple_of(tile * TILE, TILE), TILE)


def iota(axis, shape=(TILE, TILE)):
    return lax.broadcasted_iota(jnp.int32, shape, axis)


def kernel(
    scores, flips, presence, covs, membership, weights, owner, gene,
    burden_out, skat_out,
    buf, got, factor_wide, cov_in, cov_out, cov_got, factor, sign, held,
    var_mine, var_got, spread_mine, spread_got, stats, stats_got,
    wide, packed, arrived, wide_got,
    load_sem, cov_sem, send_sem, recv_sem, cov_send, cov_recv,
    var_send, var_recv, spread_send, spread_recv, stat_send, stat_recv, pay_send, pay_recv,
):
    me = lax.axis_index("cohort")
    mine = lax.axis_index("gene")

    def cohort(relative):
        return lax.rem(me + relative, COHORTS)

    def owner_at(offset):
        return lax.rem(mine + offset, OWNERS)

    def load(relative):
        columns = pl.ds(pl.multiple_of(cohort(relative) * TILE, TILE), TILE)
        return pltpu.make_async_copy(scores.at[0, :, columns], buf.at[relative], load_sem.at[relative])

    load_cov = pltpu.make_async_copy(covs.at[0], cov_in, cov_sem)
    load(2).start()
    load(1).start()
    load(3).start()
    load_cov.start()
    load(0).start()

    barrier = pltpu.get_barrier_semaphore()
    for step in range(1, COHORTS):
        pl.semaphore_signal(barrier, inc=1, device_id={"cohort": cohort(step)}, device_id_type=MESH)

    def greet(offset, carry):
        pl.semaphore_signal(barrier, inc=1, device_id={"gene": owner_at(offset)}, device_id_type=MESH)
        return carry

    lax.fori_loop(1, OWNERS, greet, 0)

    sign[...] = 1.0 - 2.0 * flips[...].astype(F32)
    factor[...] = sign[...] * presence[...].astype(F32)
    held[...] = jnp.zeros_like(held)

    owner_row = jnp.full((1, TILE), -1.0, F32)
    owner_row = jnp.concatenate([owner[...].astype(F32), owner_row[:, :TILE - TILES]], axis=1)
    gene_row = jnp.concatenate([gene[...].astype(F32) + 1.0, jnp.zeros((1, TILE - TILES), F32)], axis=1)
    owner_rows = jnp.broadcast_to(owner_row, (TILE, TILE))
    same = (owner_rows == owner_rows.T) & (iota(0) < iota(1))
    rank_row = jnp.sum(same.astype(F32), axis=0, keepdims=True)
    slot_row = jnp.where(owner_row >= 0.0, owner_row + OWNERS * rank_row, -1.0)
    slots = (slot_row == iota(0).astype(F32)).astype(F32)

    def piece(way, phase, chunk):
        half = 1 - way if phase == 1 else way
        relative = 2 if phase == 0 else (1 if way == 0 else 3)
        first = pl.multiple_of((half * HALF + chunk * CHUNK_TILES) * TILE, TILE)
        landing = pl.multiple_of(chunk * CHUNK_ROWS, TILE)
        return pltpu.make_async_remote_copy(
            src_ref=buf.at[relative, pl.ds(first, CHUNK_ROWS)],
            dst_ref=got.at[phase, way, pl.ds(landing, CHUNK_ROWS)],
            send_sem=send_sem.at[way, phase, chunk],
            recv_sem=recv_sem.at[way, phase, chunk],
            device_id={"cohort": cohort(1 if way == 0 else 3)},
            device_id_type=MESH,
        )

    def cov_piece(way, phase):
        half = 1 - way if phase == 1 else way
        relative = 2 if phase == 0 else (1 if way == 0 else 3)
        return pltpu.make_async_remote_copy(
            src_ref=cov_out.at[cohort(relative), half],
            dst_ref=cov_got.at[phase, way],
            send_sem=cov_send.at[way, phase],
            recv_sem=cov_recv.at[way, phase],
            device_id={"cohort": cohort(1 if way == 0 else 3)},
            device_id_type=MESH,
        )

    def mask_weights(tile):
        member = membership[:, rows_of(tile)].astype(F32)
        return (weights[pl.ds(tile, 1), :] * (1.0 + 3.0 * member) / 4.0).astype(BF16)

    load(2).wait()
    pl.semaphore_wait(barrier, OWNERS - 1 + COHORTS - 1)

    def far(chunk, carry):
        for way in range(2):
            def one(k, inner):
                tile = way * HALF + chunk * CHUNK_TILES + k
                rows = rows_of(tile)
                column = jnp.broadcast_to(factor[pl.ds(tile, 1), :], (TILE, TILE)).T
                factor_wide[rows, :] = column.astype(BF16)
                buf[2, rows, :] = (buf[2, rows, :].astype(F32) * column).astype(BF16)
                return inner

            lax.fori_loop(0, CHUNK_TILES, one, 0)
            piece(way, 0, chunk).start()
        return carry

    lax.fori_loop(0, CHUNKS, far, 0)

    load_cov.wait()
    lane = iota(1, (MASKS, TILE))

    def cov_group(group, linear):
        root, half = group // 2, lax.rem(group, 2)
        diagonals = jnp.zeros((16, TILE), F32)
        for k in range(PAIRS // 2):
            upper = root * OWN_TILES + half * (PAIRS // 2) + k
            signed = []
            for tile in (upper, upper + PAIRS):
                row = jnp.broadcast_to(sign[pl.ds(tile, 1), :], (TILE, TILE))
                block = cov_in[tile].astype(F32) * row * row.T
                diagonal = jnp.sum(jnp.where(iota(0) == iota(1), block, 0.0), axis=0, keepdims=True)
                w_rows = mask_weights(tile)
                w_wide = w_rows.astype(F32)
                carried = jnp.dot(w_rows, block.astype(BF16), preferred_element_type=F32)
                variance = jnp.sum(carried * w_wide, axis=1, keepdims=True)
                trace = jnp.sum(w_wide * w_wide * diagonal, axis=1, keepdims=True)
                linear = linear + jnp.where(lane == tile, variance, 0.0)
                linear = linear + jnp.where(lane == tile + 64, trace, 0.0)
                signed.append(block)
            diagonals = jnp.where(iota(0, (16, TILE)) == k, diagonal, diagonals)
            both = jnp.where(iota(0) <= iota(1), signed[0], signed[1])
            cov_out[root, half, k * TILE:(k + 1) * TILE, :] = both.astype(BF16)
        cov_out[root, half, PAIRS // 2 * TILE:, :] = diagonals.astype(BF16)
        return linear

    var_mine[...] = lax.fori_loop(0, 2 * COHORTS, cov_group, jnp.zeros((MASKS, TILE), F32))

    def to_cohorts(source, target, sent, received):
        return [
            pltpu.make_async_remote_copy(
                src_ref=source,
                dst_ref=target.at[step - 1],
                send_sem=sent.at[step - 1],
                recv_sem=received.at[step - 1],
                device_id={"cohort": cohort(step)},
                device_id_type=MESH,
            )
            for step in range(1, COHORTS)
        ]

    var_copies = to_cohorts(var_mine, var_got, var_send, var_recv)
    for copy in var_copies:
        copy.start()
    for way in range(2):
        cov_piece(way, 0).start()
        cov_piece(way, 1).start()

    load(1).wait()
    load(3).wait()

    def near(chunk, carry):
        for way in range(2):
            relative = 1 if way == 0 else 3

            def one(k, inner):
                rows = rows_of((1 - way) * HALF + chunk * CHUNK_TILES + k)
                buf[relative, rows, :] = buf[relative, rows, :] * factor_wide[rows, :]
                return inner

            lax.fori_loop(0, CHUNK_TILES, one, 0)
            piece(way, 1, chunk).start()
        return carry

    lax.fori_loop(0, CHUNKS, near, 0)

    for way in range(2):
        cov_piece(way, 0).wait_recv()
        root = cohort(1 if way == 0 else 3)
        cov_out[root, way] = (cov_out[root, way].astype(F32) + cov_got[0, way].astype(F32)).astype(BF16)
        cov_piece(way, 2).start()

    def onward(chunk, carry):
        for way in range(2):
            relative = 1 if way == 0 else 3
            piece(way, 0, chunk).wait_recv()

            def one(k, inner):
                rows = rows_of(way * HALF + chunk * CHUNK_TILES + k)
                landed = rows_of(chunk * CHUNK_TILES + k)
                term = buf[relative, rows, :].astype(F32) * factor_wide[rows, :].astype(F32)
                buf[relative, rows, :] = (term + got[0, way, landed, :].astype(F32)).astype(BF16)
                return inner

            lax.fori_loop(0, CHUNK_TILES, one, 0)
            piece(way, 2, chunk).start()
        return carry

    lax.fori_loop(0, CHUNKS, onward, 0)

    spreads = jnp.zeros((MASKS, TILE), F32)
    for half in range(2):
        cov_piece(1 - half, 1).wait_recv()
        cov_piece(half, 2).wait_recv()
        total = (
            cov_out[me, half].astype(F32)
            + cov_got[1, 1 - half].astype(F32)
            + cov_got[2, half].astype(F32)
        )
        for k in range(PAIRS // 2):
            square = total[k * TILE:(k + 1) * TILE, :]
            square = square * square
            row_at = PAIRS // 2 * TILE + k
            diagonal = total[row_at:row_at + 1, :]
            upper = jnp.where(iota(0) < iota(1), 2.0 * square, jnp.where(iota(0) == iota(1), square, 0.0))
            lower = jnp.where(iota(0) > iota(1), 2.0 * square, 0.0)
            first = me * OWN_TILES + half * (PAIRS // 2) + k
            for tile, part in ((first, upper), (first + PAIRS, lower)):
                w_wide = mask_weights(tile).astype(F32)
                w_square = w_wide * w_wide
                carried = jnp.dot(w_square, part, precision=HIGHEST, preferred_element_type=F32)
                if part is lower:
                    carried = carried + w_square * (diagonal * diagonal)
                spread = jnp.sum(carried * w_square, axis=1, keepdims=True)
                spreads = spreads + jnp.where(lane == tile, spread, 0.0)
    spread_mine[...] = spreads
    spread_copies = to_cohorts(spread_mine, spread_got, spread_send, spread_recv)
    for copy in spread_copies:
        copy.start()
    for copy in var_copies + spread_copies:
        copy.wait_recv()
    linear = var_mine[...] + var_got[0] + var_got[1] + var_got[2]
    spreads = spreads + spread_got[0] + spread_got[1] + spread_got[2]

    facts = jnp.concatenate(
        [
            jnp.where(lane < 64, linear, 0.0),
            spreads,
            jnp.broadcast_to(gene_row, (MASKS, TILE)),
            jnp.zeros((64 - 3 * MASKS, TILE), F32),
        ],
        axis=0,
    )
    slot_facts = lax.dot_general(
        slots, facts, (((1,), (1,)), ((), ())), precision=HIGHEST, preferred_element_type=F32
    )
    stats[...] = jnp.concatenate([slot_facts[:OWNERS], slot_facts[OWNERS:]], axis=1)
    stats_got[pl.ds(mine, 1), :] = stats[pl.ds(mine, 1), :]

    def send_stats(offset, carry):
        there = owner_at(offset)
        pltpu.make_async_remote_copy(
            src_ref=stats.at[pl.ds(there, 1)],
            dst_ref=stats_got.at[pl.ds(mine, 1)],
            send_sem=stat_send,
            recv_sem=stat_recv,
            device_id={"gene": there},
            device_id_type=MESH,
        ).start()
        return carry

    lax.fori_loop(1, OWNERS, send_stats, 0)

    load(0).wait()

    def finish(chunk, carry):
        for half in range(2):
            piece(1 - half, 1, chunk).wait_recv()
            piece(half, 2, chunk).wait_recv()

            def one(k, inner):
                tile = half * HALF + chunk * CHUNK_TILES + k
                rows = rows_of(tile)
                landed = rows_of(chunk * CHUNK_TILES + k)
                united = (
                    buf[0, rows, :].astype(F32) * factor_wide[rows, :].astype(F32)
                    + got[1, 1 - half, landed, :].astype(F32)
                    + got[2, half, landed, :].astype(F32)
                )
                w_rows = mask_weights(tile)
                burden = jnp.dot(w_rows, united.astype(BF16), preferred_element_type=F32)
                w_wide = w_rows.astype(F32)
                w_square = w_wide * w_wide
                w_high = w_square.astype(BF16).astype(F32)
                w_parts = jnp.concatenate([w_high, w_square - w_high], axis=0).astype(BF16)
                square = united * united
                high = square.astype(BF16)
                low = (square - high.astype(F32)).astype(BF16)
                main = jnp.dot(w_parts, high, preferred_element_type=F32)
                rest = jnp.dot(w_parts, low, preferred_element_type=F32)
                trace = jnp.sum(jnp.where(lane == tile + 64, linear, 0.0), axis=1, keepdims=True)
                total = main[:MASKS] + (main[MASKS:] + rest[:MASKS])
                first = pl.multiple_of(tile * 2 * MASKS, 2 * MASKS)
                held[pl.ds(first, MASKS), :] = burden
                held[pl.ds(first + MASKS, MASKS), :] = total - trace
                return inner

            lax.fori_loop(0, CHUNK_TILES, one, 0)
        return carry

    lax.fori_loop(0, CHUNKS, finish, 0)

    slots_narrow = slots.astype(BF16)
    for row in range(2 * MASKS):
        tiles = held[pl.ds(row, TILE, stride=2 * MASKS), :].astype(BF16)
        chosen = jnp.dot(slots_narrow, tiles, preferred_element_type=F32)
        for second in range(2):
            wide[pl.ds(second * 2 * MASKS + row, OWNERS, stride=4 * MASKS), :] = chosen[
                second * OWNERS:(second + 1) * OWNERS
            ]

    def narrow(index):
        first = pl.multiple_of(index * 4 * MASKS, 4 * MASKS)
        return wide[pl.ds(first, 4 * MASKS), :].astype(BF16)

    def send_slots(offset, carry):
        there = owner_at(offset)
        packed[there] = narrow(there)
        pltpu.make_async_remote_copy(
            src_ref=packed.at[there],
            dst_ref=arrived.at[mine],
            send_sem=pay_send,
            recv_sem=pay_recv,
            device_id={"gene": there},
            device_id_type=MESH,
        ).start()
        return carry

    lax.fori_loop(1, OWNERS, send_slots, 0)
    arrived[mine] = narrow(mine)

    pltpu.make_async_copy(stats_got.at[pl.ds(0, OWNERS - 1)], stats_got.at[pl.ds(0, OWNERS - 1)], stat_recv).wait()
    all_stats = stats_got[...]
    turned = jnp.concatenate([all_stats, jnp.zeros_like(all_stats)], axis=0).T
    gene_at = (iota(0, (GENES, OWNERS)) + 1).astype(F32)
    chosen_by = [
        (jnp.broadcast_to(turned[second * 64 + 2 * MASKS:second * 64 + 2 * MASKS + 1, :OWNERS], (GENES, OWNERS)) == gene_at)
        .astype(F32)
        for second in range(2)
    ]
    sums = [
        jnp.dot(chosen, all_stats, precision=HIGHEST, preferred_element_type=F32) for chosen in chosen_by
    ]
    moments = sums[0][:, :64] + sums[1][:, 64:]
    doubled = jnp.where(iota(1, (GENES, 64)) >= MASKS, 2.0 * moments, moments)
    scale = 1.0 / jnp.sqrt(jnp.maximum(doubled, 1.0))
    membership_of_gene = jnp.concatenate(chosen_by, axis=1).astype(BF16)

    pltpu.make_async_copy(arrived.at[pl.ds(0, OWNERS - 1)], arrived.at[pl.ds(0, OWNERS - 1)], pay_recv).wait()
    wide_got[...] = arrived[...].astype(F32).reshape(OWNERS * 4 * MASKS, TILE)
    for row in range(2 * MASKS):
        both = jnp.concatenate(
            [wide_got[pl.ds(second * 2 * MASKS + row, OWNERS, stride=4 * MASKS), :] for second in range(2)], axis=0
        ).astype(BF16)
        total = jnp.dot(membership_of_gene, both, preferred_element_type=F32)
        result = total * scale[:, row:row + 1]
        if row < MASKS:
            burden_out[:, row, :] = result
        else:
            skat_out[:, row - MASKS, :] = result

    def all_sent(chunk, carry):
        for way in range(2):
            for phase in range(3):
                piece(way, phase, chunk).wait_send()
        return carry

    lax.fori_loop(0, CHUNKS, all_sent, 0)
    for way in range(2):
        for phase in range(3):
            cov_piece(way, phase).wait_send()
    for copy in var_copies + spread_copies:
        copy.wait_send()
    pltpu.make_async_copy(stats.at[pl.ds(0, OWNERS - 1)], stats.at[pl.ds(0, OWNERS - 1)], stat_send).wait()
    pltpu.make_async_copy(packed.at[pl.ds(0, OWNERS - 1)], packed.at[pl.ds(0, OWNERS - 1)], pay_send).wait()


def shards(scores, flips, presence, covs, membership, weights, tile_owner, tile_gene):
    vmem = pl.BlockSpec(memory_space=pltpu.VMEM)
    hbm = pl.BlockSpec(memory_space=pl.ANY)
    out = jax.ShapeDtypeStruct((GENES, MASKS, TILE), F32)
    dma = pltpu.SemaphoreType.DMA
    scratch = [
        pltpu.VMEM((COHORTS, TILES * TILE, TILE), BF16),
        pltpu.VMEM((3, 2, HALF * TILE, TILE), BF16),
        pltpu.VMEM((TILES * TILE, TILE), BF16),
        pltpu.VMEM((TILES, TILE, TILE), BF16),
        pltpu.VMEM((COHORTS, 2, COV_ROWS, TILE), BF16),
        pltpu.VMEM((3, 2, COV_ROWS, TILE), BF16),
        pltpu.VMEM((TILES, TILE), F32),
        pltpu.VMEM((TILES, TILE), F32),
        pltpu.VMEM((TILE * 2 * MASKS, TILE), F32),
        pltpu.VMEM((MASKS, TILE), F32),
        pltpu.VMEM((COHORTS - 1, MASKS, TILE), F32),
        pltpu.VMEM((MASKS, TILE), F32),
        pltpu.VMEM((COHORTS - 1, MASKS, TILE), F32),
        pltpu.VMEM((OWNERS, TILE), F32),
        pltpu.VMEM((OWNERS, TILE), F32),
        pltpu.VMEM((OWNERS * 4 * MASKS, TILE), F32),
        pltpu.VMEM((OWNERS, 4 * MASKS, TILE), BF16),
        pltpu.VMEM((OWNERS, 4 * MASKS, TILE), BF16),
        pltpu.VMEM((OWNERS * 4 * MASKS, TILE), F32),
        dma((COHORTS,)),
        dma,
        dma((2, 3, CHUNKS)),
        dma((2, 3, CHUNKS)),
        dma((2, 3)),
        dma((2, 3)),
        dma((COHORTS - 1,)),
        dma((COHORTS - 1,)),
        dma((COHORTS - 1,)),
        dma((COHORTS - 1,)),
        dma,
        dma,
        dma,
        dma,
    ]
    return pl.pallas_call(
        kernel,
        out_shape=(out, out),
        in_specs=[hbm, vmem, vmem, hbm, vmem, vmem, vmem, vmem],
        out_specs=(vmem, vmem),
        scratch_shapes=scratch,
        compiler_params=pltpu.CompilerParams(
            collective_id=0, has_side_effects=True, vmem_limit_bytes=48 * 1024 * 1024
        ),
        cost_estimate=pl.CostEstimate(flops=500_000_000, bytes_accessed=9_000_000, transcendentals=0),
    )(
        scores,
        flips.reshape(TILES, TILE),
        presence.reshape(TILES, TILE),
        covs,
        membership,
        weights.reshape(TILES, TILE),
        tile_owner.reshape(1, TILES),
        tile_gene.reshape(1, TILES),
    )


def solution(mesh):
    return jax.shard_map(
        shards,
        mesh=mesh,
        in_specs=(
            P("cohort", "gene", None),
            P("cohort", "gene"),
            P("cohort", "gene"),
            P("cohort", "gene", None, None),
            P(None, "gene"),
            P("gene"),
            P("gene", None),
            P("gene"),
        ),
        out_specs=(P("gene", None, "cohort"), P("gene", None, "cohort")),
        check_vma=False,
    )
```

time: 432 us -> 105 us (0.24)
  waiting for transfers between devices: 181 us -> 0 us
  blocking collectives: 102 us -> 0 us
  Pallas kernels: 0 us -> 97.4 us
  local copies, waits for them, and re-layouts: 42.1 us -> 7.11 us
  matrix products: 32 us -> 0 us
  other arithmetic: 30 us -> 0 us
  starting transfers between devices: 29.7 us -> 0 us
  between operations: 14.3 us -> 0.66 us
    all_to_all x1 -> x0, blocking collectives: 102 us -> none  [shards(): lax.all_to_all(packed_slots(u_rows), 'gene', split_axis=0, concat_axis=0,...]
    pallas_call x0 -> x1, Pallas kernels: none -> 97.4 us  [shards(): pl.pallas_call(kernel, out_shape=(out, out), in_specs=[hbm, vmem, vmem, h...]
    all_to_all x3 -> x0, waiting for transfers between devices: 90.8 us -> none  [the longest x1 85.2 us: shards(): lax.all_to_all(packed_slots(blocks), 'gene', split_axis=0, concat_axis=0,...]
    unnamed x3 -> x0, waiting for transfers between devices: 64.9 us -> none
    dot_general x9 -> x0, matrix products: 32 us -> none  [the longest x1 15.7 us: block_moments(): jnp.einsum('kij,kmj->kmi', v_wide * v_wide, w_square, precision=lax.Preci...]
    all_to_all x3 -> x0, starting transfers between devices: 29.6 us -> none  [the longest x1 13 us: shards(): lax.all_to_all(gene_slots.astype(jnp.bfloat16), 'gene', split_axis=0, con...]
    psum x1 -> x0, waiting for transfers between devices: 24.9 us -> none  [shards(): blocks = lax.psum(cov_term.astype(jnp.bfloat16), 'cohort')]
    convert_element_type x5 -> x0, other arithmetic: 14.4 us -> none  [the longest x1 6.96 us: shards(): signed.astype(jnp.bfloat16)]
  transfers between devices with their start and end apart: 5 -> 0, of which waited for: 4 -> 0; matrix products, arithmetic and copies ran while one was open for 11% -> 0% of each run, Pallas kernels for 0% -> 0%
where the time goes in v1:
time: 105 us
  Pallas kernels  97.4 us (93%)
  local copies, waits for them, and re-layouts  7.11 us (7%)
    pallas_call x1, Pallas kernels, shards(): pl.pallas_call(kernel, out_shape=(out, out), in_specs=[hbm, vmem, vmem, h...  97.4 us
    unnamed x16, local copies, waits for them, and re-layouts  7.11 us

profile of v1, /device:TPU:1, one launch (start us, length us, event | category | flops | bytes accessed | tf_op | source)
XLA Modules:
  0.0 105.1 jit_solution(16683215456624167028)
XLA Ops:
  0.6 0.0 copy-start
  0.6 1.4 %copy-done = bf16[1,48,128,128]{3,2,1,0:T(8,128)(2,1)S(1)} copy-done((bf16[1,48,128,128]{3,2,1,0:T(8,128)(2,1)S(1)}, bf16[1,48,128,128]{3,2,1,0:T(8,128)(2,1)}, u32[]{:S(2)}) %copy-start) | copy-done | bytes 1572888
  2.0 0.0 copy-start.1
  2.0 0.9 copy-done.1
  3.0 0.0 copy-start.2
  3.0 0.7 copy-done.2
  3.7 0.0 copy-start.3
  3.7 0.7 copy-done.3
  4.4 0.0 copy-start.4
  4.4 0.7 copy-done.4
  5.2 0.0 copy-start.5
  5.2 0.7 copy-done.5
  5.8 0.0 copy-start.6
  5.8 0.7 copy-done.6
  6.5 97.4 %shard_map.95 = (f32[16,8,128]{2,1,0:T(8,128)S(1)}, f32[16,8,128]{2,1,0:T(8,128)S(1)}) custom-call(bf16[1,6144,512]{2,1,0:T(8,128)(2,1)} %scores.1, s32[48,128]{1,0:T(8,128)S(1)} %bitcast.5, s32[48,128]{1,0:T(8,128)S(1)} %bitcast.6, bf16[1,48,128,128]{3,2,1,0:T(8,128)(2,1)S(1)} %copy-done, s32[8,6144]{1,0:T(8,128)S(1)} %copy-done.1, f32[48,128]{1,0:T(8,128)S(1)} %bitcast.7, ...), custom_call_target="tpu_custom_call" | custom-call | flops 500000000 | bytes 9000000 | tf_op jit(solution)/shard_map/pallas_call | solution.py:445
  103.9 0.6 copy.12
  104.5 0.6 copy.13
Async XLA Ops:
  0.6 1.4 %copy-start = (bf16[1,48,128,128]{3,2,1,0:T(8,128)(2,1)S(1)}, bf16[1,48,128,128]{3,2,1,0:T(8,128)(2,1)}, u32[]{:S(2)}) copy-start(bf16[1,48,128,128]{3,2,1,0:T(8,128)(2,1)} %covs.1) | copy-start | bytes 4718596
  2.0 0.9 copy-start.1
  3.0 0.7 copy-start.2
  3.7 0.7 copy-start.3
  4.4 0.7 copy-start.4
  5.2 0.7 copy-start.5
  5.8 0.7 copy-start.6

commit v2 on v1

v2 whole, which is shorter than its diff:
```python
import jax
import jax.numpy as jnp
from jax import lax
from jax.experimental import pallas as pl
from jax.experimental.pallas import tpu as pltpu
from jax.sharding import PartitionSpec as P

F32, BF16 = jnp.float32, jnp.bfloat16
MESH = pl.DeviceIdType.MESH
TILE = 128
TILES = 48
PAIRED = TILES // 2
HALF = TILE // 2
GROUP = PAIRED // 2
CHUNKS = 4
SQUARES = GROUP // CHUNKS
CHUNK_ROWS = SQUARES * TILE
COHORTS = 4
OWNERS = 64
SIDE = 8
BATCH = 4
AWAY = (0, 4, 3, 5, 2, 6, 1, 7)
GENES = 16
MASKS = 8
FIELDS = 2 * MASKS
OWN_TILES = TILES // COHORTS
PAIRS = OWN_TILES // 2
COV_ROWS = PAIRS // 2 * TILE + 16
FLIGHT = 3
SELECT = 32
HIGHEST = lax.Precision.HIGHEST


def rows_of(tile, count=1):
    return pl.ds(pl.multiple_of(tile * TILE, TILE), count * TILE)


def iota(axis, shape=(TILE, TILE)):
    return lax.broadcasted_iota(jnp.int32, shape, axis)


def swap(value):
    return pltpu.roll(value, HALF, 1)


def left(shape=(TILE, TILE)):
    return iota(1, shape) < HALF


def kernel(
    scores, flips_in, presence_in, covs, membership_in, weights_in, owner_in, gene_in,
    burden_out, skat_out,
    flips, presence, membership, weights, owner, gene,
    buf, got, factor_wide, cov_in, cov_out, cov_got, factor, sign, held,
    var_mine, var_got, spread_mine, spread_got, stats, stats_got,
    stats_relayed, stats_turned, wide, packed, relayed, arrived, wide_got,
    small_sem, far_sem, load_sem, cov_sem, send_sem, recv_sem, cov_send, cov_recv,
    var_send, var_recv, spread_send, spread_recv, stat_send, stat_recv, pay_send, pay_recv, relay_send, relay_recv,
):
    me = lax.axis_index("cohort")
    mine = lax.axis_index("gene")

    def cohort(relative):
        return lax.rem(me + relative, COHORTS)

    my_z = lax.rem(mine // 2, SIDE)
    my_place = 2 * (mine // 16) + lax.rem(mine, 2)

    def along_z(offset):
        return lax.rem(my_z + offset, SIDE)

    def across(offset):
        return lax.rem(my_place + offset, SIDE)

    def owner_of(z, place):
        return 16 * (place // 2) + 2 * z + lax.rem(place, 2)

    def columns(relative):
        return pl.ds(pl.multiple_of(cohort(relative) * TILE, TILE), TILE)

    def load(relative):
        return pltpu.make_async_copy(scores.at[0, :, columns(relative)], buf.at[relative], load_sem.at[relative])

    def load_far(group, chunk, second):
        rows = rows_of(second * PAIRED + group * GROUP + chunk * SQUARES, SQUARES)
        return pltpu.make_async_copy(
            scores.at[0, rows, columns(2)], buf.at[2, rows], far_sem.at[group, chunk, second]
        )

    pieces = ((flips_in, flips), (presence_in, presence), (membership_in, membership),
              (weights_in, weights), (owner_in, owner), (gene_in, gene))
    small = [pltpu.make_async_copy(source, target, small_sem.at[i]) for i, (source, target) in enumerate(pieces)]
    load_cov = pltpu.make_async_copy(covs.at[0], cov_in, cov_sem)
    small[0].start()
    small[1].start()
    for chunk in range(CHUNKS):
        for group in range(2):
            for second in range(2):
                load_far(group, chunk, second).start()

    barrier = pltpu.get_barrier_semaphore()
    for step in range(1, COHORTS):
        pl.semaphore_signal(barrier, inc=1, device_id={"cohort": cohort(step)}, device_id_type=MESH)

    for offset in range(1, SIDE):
        for there in (owner_of(along_z(offset), my_place), owner_of(my_z, across(offset))):
            pl.semaphore_signal(barrier, inc=1, device_id={"gene": there}, device_id_type=MESH)
    load(1).start()
    load(3).start()
    for copy in small[2:]:
        copy.start()
    load_cov.start()
    load(0).start()

    def piece(way, phase, part, chunk):
        group = 1 - way if phase == 1 else way
        relative = 2 if phase == 0 else (1 if way == 0 else 3)
        return pltpu.make_async_remote_copy(
            src_ref=buf.at[relative, rows_of(part * PAIRED + group * GROUP + chunk * SQUARES, SQUARES)],
            dst_ref=got.at[phase, way, rows_of(part * GROUP + chunk * SQUARES, SQUARES)],
            send_sem=send_sem.at[way, phase, part, chunk],
            recv_sem=recv_sem.at[way, phase, part, chunk],
            device_id={"cohort": cohort(1 if way == 0 else 3)},
            device_id_type=MESH,
        )

    def cov_piece(way, phase):
        half = 1 - way if phase == 1 else way
        relative = 2 if phase == 0 else (1 if way == 0 else 3)
        return pltpu.make_async_remote_copy(
            src_ref=cov_out.at[cohort(relative), half],
            dst_ref=cov_got.at[phase, way],
            send_sem=cov_send.at[way, phase],
            recv_sem=cov_recv.at[way, phase],
            device_id={"cohort": cohort(1 if way == 0 else 3)},
            device_id_type=MESH,
        )

    def pair_up(relative, square):
        first, second = rows_of(square), rows_of(square + PAIRED)
        x = buf[relative, first, :].astype(F32)
        y = buf[relative, second, :].astype(F32)
        sign_of = factor_wide[first, :].astype(F32)
        buf[relative, first, :] = (jnp.where(left(), x, swap(y)) * sign_of).astype(BF16)
        buf[relative, second, :] = (jnp.where(left(), swap(x), y) * sign_of).astype(BF16)

    def mask_weights(tile):
        member = membership[:, rows_of(tile)].astype(F32)
        return (weights[pl.ds(tile, 1), :] * (1.0 + 3.0 * member) / 4.0).astype(BF16)

    small[0].wait()
    small[1].wait()
    sign[...] = 1.0 - 2.0 * flips[...].astype(F32)
    factor[...] = sign[...] * presence[...].astype(F32)

    def far(group, chunk):
        load_far(group, chunk, 0).wait()
        load_far(group, chunk, 1).wait()

        def one(k, inner):
            square = group * GROUP + chunk * SQUARES + k
            x = jnp.broadcast_to(factor[pl.ds(square, 1), :], (TILE, TILE)).T
            y = jnp.broadcast_to(factor[pl.ds(square + PAIRED, 1), :], (TILE, TILE)).T
            factor_wide[rows_of(square), :] = jnp.where(left(), x, y).astype(BF16)
            pair_up(2, square)
            return inner

        lax.fori_loop(0, SQUARES, one, 0, unroll=True)

    far(0, 0)
    far(1, 0)
    pl.semaphore_wait(barrier, 2 * (SIDE - 1) + COHORTS - 1)
    piece(0, 0, 0, 0).start()
    piece(1, 0, 0, 0).start()

    def more_far(chunk, carry):
        for way in range(2):
            far(way, chunk)
            piece(way, 0, 0, chunk).start()
        return carry

    lax.fori_loop(1, CHUNKS, more_far, 0)

    for copy in small[2:]:
        copy.wait()
    load_cov.wait()
    lane = iota(1, (MASKS, TILE))

    def cov_group(group, linear):
        root, half = group // 2, lax.rem(group, 2)
        diagonals = jnp.zeros((16, TILE), F32)
        for k in range(PAIRS // 2):
            upper = root * OWN_TILES + half * (PAIRS // 2) + k
            signed = []
            for tile in (upper, upper + PAIRS):
                row = jnp.broadcast_to(sign[pl.ds(tile, 1), :], (TILE, TILE))
                block = cov_in[tile].astype(F32) * row * row.T
                diagonal = jnp.sum(jnp.where(iota(0) == iota(1), block, 0.0), axis=0, keepdims=True)
                w_rows = mask_weights(tile)
                w_wide = w_rows.astype(F32)
                carried = jnp.dot(w_rows, block.astype(BF16), preferred_element_type=F32)
                variance = jnp.sum(carried * w_wide, axis=1, keepdims=True)
                trace = jnp.sum(w_wide * w_wide * diagonal, axis=1, keepdims=True)
                linear = linear + jnp.where(lane == tile, variance, 0.0)
                linear = linear + jnp.where(lane == tile + 64, trace, 0.0)
                signed.append(block)
            diagonals = jnp.where(iota(0, (16, TILE)) == k, diagonal, diagonals)
            both = jnp.where(iota(0) <= iota(1), signed[0], signed[1])
            cov_out[root, half, k * TILE:(k + 1) * TILE, :] = both.astype(BF16)
        cov_out[root, half, PAIRS // 2 * TILE:, :] = diagonals.astype(BF16)
        return linear

    var_mine[...] = lax.fori_loop(0, 2 * COHORTS, cov_group, jnp.zeros((MASKS, TILE), F32))

    def to_cohorts(source, target, sent, received):
        return [
            pltpu.make_async_remote_copy(
                src_ref=source,
                dst_ref=target.at[step - 1],
                send_sem=sent.at[step - 1],
                recv_sem=received.at[step - 1],
                device_id={"cohort": cohort(step)},
                device_id_type=MESH,
            )
            for step in range(1, COHORTS)
        ]

    var_copies = to_cohorts(var_mine, var_got, var_send, var_recv)
    for copy in var_copies:
        copy.start()

    chunks = range(CHUNKS)
    order = [(0, 0, c) for c in chunks] + [(1, 0, c) for c in chunks] + [(0, None, 0), (1, None, 0)]
    order += [(2, 0, c) for c in chunks] + [(2, None, 0)]
    order += [(phase, 1, c) for phase in range(3) for c in chunks]

    def copy_of(item, way):
        phase, part, chunk = item
        return cov_piece(way, phase) if part is None else piece(way, phase, part, chunk)

    def prepare(item, way):
        phase, part, chunk = item
        relative = 1 if way == 0 else 3
        if part is None and phase == 2:
            cov_piece(way, 0).wait_recv()
            root = cohort(relative)
            cov_out[root, way] = (cov_out[root, way].astype(F32) + cov_got[0, way].astype(F32)).astype(BF16)
        elif part == 0 and phase == 1:
            for k in range(SQUARES):
                pair_up(relative, (1 - way) * GROUP + chunk * SQUARES + k)
        elif part is not None and phase == 2:
            piece(way, 0, part, chunk).wait_recv()
            for k in range(SQUARES):
                rows = rows_of(part * PAIRED + way * GROUP + chunk * SQUARES + k)
                landed = rows_of(part * GROUP + chunk * SQUARES + k)
                if part == 0:
                    pair_up(relative, way * GROUP + chunk * SQUARES + k)
                total = buf[relative, rows, :].astype(F32) + got[0, way, landed, :].astype(F32)
                buf[relative, rows, :] = total.astype(BF16)

    def send_up_to(first, end):
        for index in range(first, end):
            for way in range(2):
                prepare(order[index], way)
                copy_of(order[index - FLIGHT], way).wait_send()
                copy_of(order[index], way).start()

    load(1).wait()
    load(3).wait()
    for item in order[:CHUNKS - FLIGHT]:
        for way in range(2):
            copy_of(item, way).wait_send()
    send_up_to(CHUNKS, 17)

    padding = jnp.full((1, TILE - TILES), -1.0, F32)
    owner_row = jnp.concatenate([owner[...].astype(F32), padding], axis=1)
    gene_row = jnp.concatenate([gene[...].astype(F32), padding], axis=1) + 1.0
    owner_rows = jnp.broadcast_to(owner_row, (TILE, TILE))
    same = (owner_rows == owner_rows.T) & (iota(0) < iota(1))
    rank_row = jnp.sum(same.astype(F32), axis=0, keepdims=True)
    owner_int = owner[...]
    place_int = 8 * ((owner_int >> 1) & 7) + 2 * (owner_int >> 4) + (owner_int & 1)
    place_row = jnp.concatenate([place_int.astype(F32), padding], axis=1)
    slot_row = jnp.where(place_row >= 0.0, place_row + OWNERS * rank_row, -1.0)
    slots = (slot_row == iota(0).astype(F32)).astype(F32)
    selector = jnp.concatenate(
        [slots[:, :SELECT], pltpu.roll(slots, TILE - PAIRED, 1)[:, :SELECT]], axis=0
    ).astype(BF16)

    load(0).wait()

    def own(index, carry):
        for group in range(2):
            pair_up(0, group * GROUP + index)
        return carry

    lax.fori_loop(0, GROUP, own, 0)

    for copy in var_copies:
        copy.wait_recv()
    linear = var_mine[...] + var_got[0] + var_got[1] + var_got[2]
    held[pl.ds(PAIRED * FIELDS, (SELECT - PAIRED) * FIELDS), :] = jnp.zeros(
        ((SELECT - PAIRED) * FIELDS, TILE), F32
    )

    def by_half(rows, count):
        parts = [rows[i * MASKS:(i + 1) * MASKS] for i in range(count)]
        return [jnp.where(left((MASKS, TILE)), parts[i], parts[i + 1]) for i in range(0, count, 2)]

    def finish(part):
        def step(chunk, carry):
            for group in range(2):
                piece(1 - group, 1, part, chunk).wait_recv()
                piece(group, 2, part, chunk).wait_recv()

                def one(k, inner):
                    square = group * GROUP + chunk * SQUARES + k
                    landed = rows_of(part * GROUP + chunk * SQUARES + k)
                    united = (
                        buf[0, rows_of(part * PAIRED + square), :].astype(F32)
                        + got[1, 1 - group, landed, :].astype(F32)
                        + got[2, group, landed, :].astype(F32)
                    )
                    w_wide = jnp.concatenate([mask_weights(square), mask_weights(square + PAIRED)], axis=0).astype(F32)
                    w_square = w_wide * w_wide
                    w_high = w_square.astype(BF16).astype(F32)
                    w_parts = jnp.concatenate([w_high, w_square - w_high], axis=0).astype(BF16)
                    squared = united * united
                    high = squared.astype(BF16)
                    low = (squared - high.astype(F32)).astype(BF16)
                    (burden,) = by_half(
                        jnp.dot(w_wide.astype(BF16), united.astype(BF16), preferred_element_type=F32), 2
                    )
                    main = by_half(jnp.dot(w_parts, high, preferred_element_type=F32), 4)
                    rest = by_half(jnp.dot(w_parts, low, preferred_element_type=F32), 4)
                    trace = [
                        jnp.sum(jnp.where(lane == tile + 64, linear, 0.0), axis=1, keepdims=True)
                        for tile in (square, square + PAIRED)
                    ]
                    traces = jnp.where(left((MASKS, TILE)), trace[0], trace[1])
                    first = pl.multiple_of(square * FIELDS, FIELDS)
                    held[pl.ds(first, MASKS), :] = burden
                    held[pl.ds(first + MASKS, MASKS), :] = main[0] + (main[1] + rest[0]) - traces
                    return inner

                lax.fori_loop(0, SQUARES, one, 0, unroll=True)
            return carry

        lax.fori_loop(0, CHUNKS, step, 0)

    def payload(part):
        for row in range(FIELDS):
            tiles = held[pl.ds(row, SELECT, stride=FIELDS), :].astype(BF16)
            chosen = jnp.dot(selector, tiles, preferred_element_type=F32)
            near_tiles, far_tiles = chosen[:TILE], chosen[TILE:]
            wide[pl.ds(row, OWNERS, stride=FIELDS), :] = jnp.where(
                left((OWNERS, TILE)),
                near_tiles[:OWNERS] + swap(far_tiles[:OWNERS]),
                swap(near_tiles[OWNERS:]) + far_tiles[OWNERS:],
            )
        packed[part] = wide[...].astype(BF16).reshape(SIDE, SIDE, FIELDS, TILE)
        for k in range(1, SIDE):
            first_stage(part, k).start()
        relayed[part, 0] = packed[part, my_z]

    def first_stage(part, k):
        there = along_z(AWAY[k])
        return pltpu.make_async_remote_copy(
            src_ref=packed.at[part, there],
            dst_ref=relayed.at[part, k],
            send_sem=pay_send.at[part, k],
            recv_sem=pay_recv.at[part, k],
            device_id={"gene": owner_of(there, my_place)},
            device_id_type=MESH,
        )

    def second_stage(part, batch, k):
        there = across(k)
        rows = pl.ds(batch * BATCH, BATCH)
        return pltpu.make_async_remote_copy(
            src_ref=relayed.at[part, rows, there],
            dst_ref=arrived.at[part, k, rows],
            send_sem=relay_send.at[part, batch, k],
            recv_sem=relay_recv.at[part, batch, k],
            device_id={"gene": owner_of(my_z, there)},
            device_id_type=MESH,
        )

    def relay(part):
        for batch in range(SIDE // BATCH):
            for k in range(max(1, batch * BATCH), (batch + 1) * BATCH):
                first_stage(part, k).wait_recv()
            for k in range(1, SIDE):
                second_stage(part, batch, k).start()
            rows = slice(batch * BATCH, (batch + 1) * BATCH)
            arrived[part, 0, rows] = relayed[part, rows, my_place]

    finish(0)
    payload(0)
    send_up_to(17, 19)

    spreads = jnp.zeros((MASKS, TILE), F32)
    for half in range(2):
        cov_piece(1 - half, 1).wait_recv()
        cov_piece(half, 2).wait_recv()
        total = (
            cov_out[me, half].astype(F32)
            + cov_got[1, 1 - half].astype(F32)
            + cov_got[2, half].astype(F32)
        )
        for k in range(PAIRS // 2):
            square = total[k * TILE:(k + 1) * TILE, :]
            square = square * square
            row_at = PAIRS // 2 * TILE + k
            diagonal = total[row_at:row_at + 1, :]
            upper = jnp.where(iota(0) < iota(1), 2.0 * square, jnp.where(iota(0) == iota(1), square, 0.0))
            lower = jnp.where(iota(0) > iota(1), 2.0 * square, 0.0)
            first = me * OWN_TILES + half * (PAIRS // 2) + k
            for tile, part in ((first, upper), (first + PAIRS, lower)):
                w_wide = mask_weights(tile).astype(F32)
                w_square = w_wide * w_wide
                carried = jnp.dot(w_square, part, precision=HIGHEST, preferred_element_type=F32)
                if part is lower:
                    carried = carried + w_square * (diagonal * diagonal)
                spread = jnp.sum(carried * w_square, axis=1, keepdims=True)
                spreads = spreads + jnp.where(lane == tile, spread, 0.0)
    spread_mine[...] = spreads
    spread_copies = to_cohorts(spread_mine, spread_got, spread_send, spread_recv)
    for copy in spread_copies:
        copy.start()
    send_up_to(19, 20)
    relay(0)
    send_up_to(20, 21)
    for copy in spread_copies:
        copy.wait_recv()
    spreads = spreads + spread_got[0] + spread_got[1] + spread_got[2]

    facts = jnp.concatenate(
        [
            jnp.where(lane < 64, linear, 0.0),
            spreads,
            jnp.broadcast_to(gene_row, (MASKS, TILE)),
            jnp.zeros((64 - 3 * MASKS, TILE), F32),
        ],
        axis=0,
    )
    slot_facts = lax.dot_general(
        slots, facts, (((1,), (1,)), ((), ())), precision=HIGHEST, preferred_element_type=F32
    )
    stats[...] = jnp.concatenate([slot_facts[:OWNERS], slot_facts[OWNERS:]], axis=1).reshape(SIDE, SIDE, TILE)

    def first_stats(k):
        there = along_z(AWAY[k])
        return pltpu.make_async_remote_copy(
            src_ref=stats.at[there],
            dst_ref=stats_relayed.at[k],
            send_sem=stat_send.at[0, k],
            recv_sem=stat_recv.at[0, k],
            device_id={"gene": owner_of(there, my_place)},
            device_id_type=MESH,
        )

    def second_stats(k):
        there = across(k)
        return pltpu.make_async_remote_copy(
            src_ref=stats_turned.at[there],
            dst_ref=stats_got.at[k],
            send_sem=stat_send.at[1, k],
            recv_sem=stat_recv.at[1, k],
            device_id={"gene": owner_of(my_z, there)},
            device_id_type=MESH,
        )

    for k in range(1, SIDE):
        first_stats(k).start()
    stats_relayed[0] = stats[my_z]
    send_up_to(21, 22)
    for k in range(1, SIDE):
        first_stats(k).wait_recv()
    for place in range(SIDE):
        stats_turned[place] = stats_relayed[:, place, :]
    for k in range(1, SIDE):
        second_stats(k).start()
    stats_got[0] = stats_turned[my_place]

    send_up_to(22, len(order))
    finish(1)
    payload(1)

    for k in range(1, SIDE):
        second_stats(k).wait_recv()
    all_stats = stats_got[...].reshape(OWNERS, TILE)
    turned = jnp.concatenate([all_stats, jnp.zeros_like(all_stats)], axis=0).T
    gene_at = (iota(0, (GENES, OWNERS)) + 1).astype(F32)
    chosen_by = jnp.concatenate(
        [
            jnp.where(
                jnp.broadcast_to(turned[row:row + 1, :OWNERS], (GENES, OWNERS)) == gene_at, 1.0, 0.0
            )
            for row in (FIELDS, 64 + FIELDS)
        ],
        axis=0,
    )
    sums = jnp.dot(chosen_by, all_stats, precision=HIGHEST, preferred_element_type=F32)
    moments = sums[:GENES, :64] + sums[GENES:, 64:]
    doubled = jnp.where(iota(1, (GENES, 64)) >= MASKS, 2.0 * moments, moments)
    scale = 1.0 / jnp.sqrt(jnp.maximum(doubled, 1.0))
    chosen_by = chosen_by.astype(BF16)

    def gather(part):
        for batch in range(SIDE // BATCH):
            for k in range(1, SIDE):
                second_stage(part, batch, k).wait_recv()
        wide_got[...] = arrived[part].astype(F32).reshape(OWNERS * FIELDS, TILE)
        results = []
        for row in range(FIELDS):
            received = wide_got[pl.ds(row, OWNERS, stride=FIELDS), :].astype(BF16)
            both = jnp.dot(chosen_by, received, preferred_element_type=F32)
            if part == 0:
                total = both[:GENES] + swap(both[GENES:])
            else:
                total = swap(both[:GENES]) + both[GENES:]
            results.append(total * scale[:, row:row + 1])
        return results

    firsts = gather(0)
    for row in range(FIELDS):
        target = burden_out if row < MASKS else skat_out
        target[:, row % MASKS, :] = firsts[row]

    relay(1)
    seconds = gather(1)
    for row in range(FIELDS):
        target = burden_out if row < MASKS else skat_out
        target[:, row % MASKS, :] = jnp.where(left((GENES, TILE)), target[:, row % MASKS, :], seconds[row])

    for item in order[-FLIGHT:]:
        for way in range(2):
            copy_of(item, way).wait_send()
    for copy in var_copies + spread_copies:
        copy.wait_send()
    for k in range(1, SIDE):
        first_stats(k).wait_send()
        second_stats(k).wait_send()
        for part in range(2):
            first_stage(part, k).wait_send()
            for batch in range(SIDE // BATCH):
                second_stage(part, batch, k).wait_send()


def shards(scores, flips, presence, covs, membership, weights, tile_owner, tile_gene):
    vmem = pl.BlockSpec(memory_space=pltpu.VMEM)
    hbm = pl.BlockSpec(memory_space=pl.ANY)
    out = jax.ShapeDtypeStruct((GENES, MASKS, TILE), F32)
    dma = pltpu.SemaphoreType.DMA
    I32 = jnp.int32
    scratch = [
        pltpu.VMEM((TILES, TILE), I32),
        pltpu.VMEM((TILES, TILE), I32),
        pltpu.VMEM((MASKS, TILES * TILE), I32),
        pltpu.VMEM((TILES, TILE), F32),
        pltpu.VMEM((1, TILES), I32),
        pltpu.VMEM((1, TILES), I32),
        pltpu.VMEM((COHORTS, TILES * TILE, TILE), BF16),
        pltpu.VMEM((3, 2, 2 * GROUP * TILE, TILE), BF16),
        pltpu.VMEM((PAIRED * TILE, TILE), BF16),
        pltpu.VMEM((TILES, TILE, TILE), BF16),
        pltpu.VMEM((COHORTS, 2, COV_ROWS, TILE), BF16),
        pltpu.VMEM((3, 2, COV_ROWS, TILE), BF16),
        pltpu.VMEM((TILES, TILE), F32),
        pltpu.VMEM((TILES, TILE), F32),
        pltpu.VMEM((SELECT * FIELDS, TILE), F32),
        pltpu.VMEM((MASKS, TILE), F32),
        pltpu.VMEM((COHORTS - 1, MASKS, TILE), F32),
        pltpu.VMEM((MASKS, TILE), F32),
        pltpu.VMEM((COHORTS - 1, MASKS, TILE), F32),
        pltpu.VMEM((SIDE, SIDE, TILE), F32),
        pltpu.VMEM((SIDE, SIDE, TILE), F32),
        pltpu.VMEM((SIDE, SIDE, TILE), F32),
        pltpu.VMEM((SIDE, SIDE, TILE), F32),
        pltpu.VMEM((OWNERS * FIELDS, TILE), F32),
        pltpu.VMEM((2, SIDE, SIDE, FIELDS, TILE), BF16),
        pltpu.VMEM((2, SIDE, SIDE, FIELDS, TILE), BF16),
        pltpu.VMEM((2, SIDE, SIDE, FIELDS, TILE), BF16),
        pltpu.VMEM((OWNERS * FIELDS, TILE), F32),
        dma((6,)),
        dma((2, CHUNKS, 2)),
        dma((COHORTS,)),
        dma,
        dma((2, 3, 2, CHUNKS)),
        dma((2, 3, 2, CHUNKS)),
        dma((2, 3)),
        dma((2, 3)),
        dma((COHORTS - 1,)),
        dma((COHORTS - 1,)),
        dma((COHORTS - 1,)),
        dma((COHORTS - 1,)),
        dma((2, SIDE)),
        dma((2, SIDE)),
        dma((2, SIDE)),
        dma((2, SIDE)),
        dma((2, SIDE // BATCH, SIDE)),
        dma((2, SIDE // BATCH, SIDE)),
    ]
    return pl.pallas_call(
        kernel,
        out_shape=(out, out),
        in_specs=[hbm] * 8,
        out_specs=(vmem, vmem),
        scratch_shapes=scratch,
        compiler_params=pltpu.CompilerParams(
            collective_id=0, has_side_effects=True, vmem_limit_bytes=48 * 1024 * 1024
        ),
        cost_estimate=pl.CostEstimate(flops=500_000_000, bytes_accessed=9_000_000, transcendentals=0),
    )(
        scores,
        flips.reshape(TILES, TILE),
        presence.reshape(TILES, TILE),
        covs,
        membership,
        weights.reshape(TILES, TILE),
        tile_owner.reshape(1, TILES),
        tile_gene.reshape(1, TILES),
    )


def solution(mesh):
    return jax.shard_map(
        shards,
        mesh=mesh,
        in_specs=(
            P("cohort", "gene", None),
            P("cohort", "gene"),
            P("cohort", "gene"),
            P("cohort", "gene", None, None),
            P(None, "gene"),
            P("gene"),
            P("gene", None),
            P("gene"),
        ),
        out_specs=(P("gene", None, "cohort"), P("gene", None, "cohort")),
        check_vma=False,
    )
```

time: 105 us -> 92.6 us (0.88)
  Pallas kernels: 97.4 us -> 84.5 us
    pallas_call x1, Pallas kernels: 97.4 us -> 84.5 us  [shards(): pl.pallas_call(kernel, out_shape=(out, out), in_specs=[hbm] * 8, out_spec...]
where the time goes in v2:
time: 92.6 us; the launch traced here: 92.3 us
  Pallas kernels  84.5 us (91%)
  local copies, waits for them, and re-layouts  7.11 us (8%)
    pallas_call x1, Pallas kernels, shards(): pl.pallas_call(kernel, out_shape=(out, out), in_specs=[hbm] * 8, out_spec...  84.5 us
    unnamed x16, local copies, waits for them, and re-layouts  7.11 us

profile of v2, /device:TPU:1, one launch (start us, length us, event | category | flops | bytes accessed | tf_op | source)
XLA Modules:
  0.0 92.3 jit_solution(1428877197207950725)
XLA Ops:
  0.6 0.0 copy-start
  0.6 1.4 %copy-done = bf16[1,48,128,128]{3,2,1,0:T(8,128)(2,1)S(1)} copy-done((bf16[1,48,128,128]{3,2,1,0:T(8,128)(2,1)S(1)}, bf16[1,48,128,128]{3,2,1,0:T(8,128)(2,1)}, u32[]{:S(2)}) %copy-start) | copy-done | bytes 1572888
  2.0 0.0 copy-start.1
  2.0 0.9 %copy-done.1 = s32[8,6144]{1,0:T(8,128)S(1)} copy-done((s32[8,6144]{1,0:T(8,128)S(1)}, s32[8,6144]{1,0:T(8,128)}, u32[]{:S(2)}) %copy-start.1) | copy-done | bytes 196632
  3.0 0.0 copy-start.2
  3.0 0.7 copy-done.2
  3.7 0.0 copy-start.3
  3.7 0.7 copy-done.3
  4.4 0.0 copy-start.4
  4.4 0.7 copy-done.4
  5.2 0.0 copy-start.5
  5.2 0.7 copy-done.5
  5.8 0.0 copy-start.6
  5.8 0.7 copy-done.6
  6.5 84.5 %shard_map.95 = (f32[16,8,128]{2,1,0:T(8,128)S(1)}, f32[16,8,128]{2,1,0:T(8,128)S(1)}) custom-call(bf16[1,6144,512]{2,1,0:T(8,128)(2,1)} %scores.1, s32[48,128]{1,0:T(8,128)S(1)} %bitcast.5, s32[48,128]{1,0:T(8,128)S(1)} %bitcast.6, bf16[1,48,128,128]{3,2,1,0:T(8,128)(2,1)S(1)} %copy-done, s32[8,6144]{1,0:T(8,128)S(1)} %copy-done.1, f32[48,128]{1,0:T(8,128)S(1)} %bitcast.7, ...), custom_call_target="tpu_custom_call" | custom-call | flops 500000000 | bytes 9000000 | tf_op jit(solution)/shard_map/pallas_call | solution.py:605
  91.0 0.6 copy.12
  91.7 0.6 copy.13
Async XLA Ops:
  0.6 1.4 %copy-start = (bf16[1,48,128,128]{3,2,1,0:T(8,128)(2,1)S(1)}, bf16[1,48,128,128]{3,2,1,0:T(8,128)(2,1)}, u32[]{:S(2)}) copy-start(bf16[1,48,128,128]{3,2,1,0:T(8,128)(2,1)} %covs.1) | copy-start | bytes 4718596
  2.0 0.9 %copy-start.1 = (s32[8,6144]{1,0:T(8,128)S(1)}, s32[8,6144]{1,0:T(8,128)}, u32[]{:S(2)}) copy-start(s32[8,6144]{1,0:T(8,128)} %membership_in.1) | copy-start | bytes 589828
  3.0 0.7 copy-start.2
  3.7 0.7 copy-start.3
  4.4 0.7 copy-start.4
  5.2 0.7 copy-start.5
  5.8 0.7 copy-start.6

commit v3 on v2

--- a/solution.py
+++ b/solution.py
@@ -91,6 +91,13 @@
               (weights_in, weights), (owner_in, owner), (gene_in, gene))
     small = [pltpu.make_async_copy(source, target, small_sem.at[i]) for i, (source, target) in enumerate(pieces)]
     load_cov = pltpu.make_async_copy(covs.at[0], cov_in, cov_sem)
+    barrier = pltpu.get_barrier_semaphore()
+    for step in range(1, COHORTS):
+        pl.semaphore_signal(barrier, inc=1, device_id={"cohort": cohort(step)}, device_id_type=MESH)
+
+    for offset in range(1, SIDE):
+        for there in (owner_of(along_z(offset), my_place), owner_of(my_z, across(offset))):
+            pl.semaphore_signal(barrier, inc=1, device_id={"gene": there}, device_id_type=MESH)
     small[0].start()
     small[1].start()
     for chunk in range(CHUNKS):
@@ -98,13 +105,6 @@
             for second in range(2):
                 load_far(group, chunk, second).start()
 
-    barrier = pltpu.get_barrier_semaphore()
-    for step in range(1, COHORTS):
-        pl.semaphore_signal(barrier, inc=1, device_id={"cohort": cohort(step)}, device_id_type=MESH)
-
-    for offset in range(1, SIDE):
-        for there in (owner_of(along_z(offset), my_place), owner_of(my_z, across(offset))):
-            pl.semaphore_signal(barrier, inc=1, device_id={"gene": there}, device_id_type=MESH)
     load(1).start()
     load(3).start()
     for copy in small[2:]:
@@ -609,7 +609,7 @@
         out_specs=(vmem, vmem),
         scratch_shapes=scratch,
         compiler_params=pltpu.CompilerParams(
-            collective_id=0, has_side_effects=True, vmem_limit_bytes=48 * 1024 * 1024
+            collective_id=0, has_side_effects=True, vmem_limit_bytes=56 * 1024 * 1024
         ),
         cost_estimate=pl.CostEstimate(flops=500_000_000, bytes_accessed=9_000_000, transcendentals=0),
     )(

time: 92.6 us -> 89.1 us (0.962)
  local copies, waits for them, and re-layouts: 7.11 us -> 2.95 us
    unnamed x16 -> x2, local copies, waits for them, and re-layouts: 7.11 us -> 2.95 us
where the time goes in v3:
time: 89.1 us; the launch traced here: 88.9 us
  Pallas kernels  85.4 us (96%)
  local copies, waits for them, and re-layouts  2.95 us (3%)
    pallas_call x1, Pallas kernels, shards(): pl.pallas_call(kernel, out_shape=(out, out), in_specs=[hbm] * 8, out_spec...  85.4 us
    unnamed x2, local copies, waits for them, and re-layouts  2.95 us

profile of v3, /device:TPU:1, one launch (start us, length us, event | category | flops | bytes accessed | tf_op | source)
XLA Modules:
  0.0 88.9 jit_solution(11262409052868824011)
XLA Ops:
  0.6 85.4 %shard_map.95 = (f32[16,8,128]{2,1,0:T(8,128)}, f32[16,8,128]{2,1,0:T(8,128)}) custom-call(bf16[1,6144,512]{2,1,0:T(8,128)(2,1)} %scores.1, s32[48,128]{1,0:T(8,128)} %bitcast.5, s32[48,128]{1,0:T(8,128)} %bitcast.6, bf16[1,48,128,128]{3,2,1,0:T(8,128)(2,1)} %covs.1, s32[8,6144]{1,0:T(8,128)} %membership_in.1, f32[48,128]{1,0:T(8,128)} %bitcast.7, ...), custom_call_target="tpu_custom_call" | custom-call | flops 500000000 | bytes 9000000 | tf_op jit(solution)/shard_map/pallas_call | solution.py:605
  86.0 1.5 %copy.12 = f32[16,8,128]{2,1,0:T(8,128)} copy(f32[16,8,128]{2,1,0:T(8,128)} %get-tuple-element.4) | data formatting | bytes 131072
  87.5 1.5 %copy.13 = f32[16,8,128]{2,1,0:T(8,128)} copy(f32[16,8,128]{2,1,0:T(8,128)} %get-tuple-element.5) | data formatting | bytes 131072

commit v4 on v3

--- a/solution.py
+++ b/solution.py
@@ -313,37 +313,38 @@
                 piece(1 - group, 1, part, chunk).wait_recv()
                 piece(group, 2, part, chunk).wait_recv()
 
-                def one(k, inner):
-                    square = group * GROUP + chunk * SQUARES + k
-                    landed = rows_of(part * GROUP + chunk * SQUARES + k)
-                    united = (
-                        buf[0, rows_of(part * PAIRED + square), :].astype(F32)
-                        + got[1, 1 - group, landed, :].astype(F32)
-                        + got[2, group, landed, :].astype(F32)
-                    )
-                    w_wide = jnp.concatenate([mask_weights(square), mask_weights(square + PAIRED)], axis=0).astype(F32)
-                    w_square = w_wide * w_wide
-                    w_high = w_square.astype(BF16).astype(F32)
-                    w_parts = jnp.concatenate([w_high, w_square - w_high], axis=0).astype(BF16)
-                    squared = united * united
-                    high = squared.astype(BF16)
-                    low = (squared - high.astype(F32)).astype(BF16)
-                    (burden,) = by_half(
-                        jnp.dot(w_wide.astype(BF16), united.astype(BF16), preferred_element_type=F32), 2
-                    )
-                    main = by_half(jnp.dot(w_parts, high, preferred_element_type=F32), 4)
-                    rest = by_half(jnp.dot(w_parts, low, preferred_element_type=F32), 4)
-                    trace = [
-                        jnp.sum(jnp.where(lane == tile + 64, linear, 0.0), axis=1, keepdims=True)
-                        for tile in (square, square + PAIRED)
-                    ]
-                    traces = jnp.where(left((MASKS, TILE)), trace[0], trace[1])
-                    first = pl.multiple_of(square * FIELDS, FIELDS)
-                    held[pl.ds(first, MASKS), :] = burden
-                    held[pl.ds(first + MASKS, MASKS), :] = main[0] + (main[1] + rest[0]) - traces
-                    return inner
-
-                lax.fori_loop(0, SQUARES, one, 0, unroll=True)
+            def one(group, k):
+                square = group * GROUP + chunk * SQUARES + k
+                landed = rows_of(part * GROUP + chunk * SQUARES + k)
+                united = (
+                    buf[0, rows_of(part * PAIRED + square), :].astype(F32)
+                    + got[1, 1 - group, landed, :].astype(F32)
+                    + got[2, group, landed, :].astype(F32)
+                )
+                w_wide = jnp.concatenate([mask_weights(square), mask_weights(square + PAIRED)], axis=0).astype(F32)
+                w_square = w_wide * w_wide
+                w_high = w_square.astype(BF16).astype(F32)
+                w_parts = jnp.concatenate([w_high, w_square - w_high], axis=0).astype(BF16)
+                squared = united * united
+                high = squared.astype(BF16)
+                low = (squared - high.astype(F32)).astype(BF16)
+                (burden,) = by_half(
+                    jnp.dot(w_wide.astype(BF16), united.astype(BF16), preferred_element_type=F32), 2
+                )
+                main = by_half(jnp.dot(w_parts, high, preferred_element_type=F32), 4)
+                rest = by_half(jnp.dot(w_parts, low, preferred_element_type=F32), 4)
+                trace = [
+                    jnp.sum(jnp.where(lane == tile + 64, linear, 0.0), axis=1, keepdims=True)
+                    for tile in (square, square + PAIRED)
+                ]
+                traces = jnp.where(left((MASKS, TILE)), trace[0], trace[1])
+                first = pl.multiple_of(square * FIELDS, FIELDS)
+                held[pl.ds(first, MASKS), :] = burden
+                held[pl.ds(first + MASKS, MASKS), :] = main[0] + (main[1] + rest[0]) - traces
+
+            for k in range(SQUARES):
+                for group in range(2):
+                    one(group, k)
             return carry
 
         lax.fori_loop(0, CHUNKS, step, 0)

time: 89.1 us -> 89 us (level)
  no operation moved by 1% of the time
where the time goes in v4:
time: 89 us; the launch traced here: 88.8 us
  Pallas kernels  85.2 us (96%)
  local copies, waits for them, and re-layouts  2.95 us (3%)
    pallas_call x1, Pallas kernels, shards(): pl.pallas_call(kernel, out_shape=(out, out), in_specs=[hbm] * 8, out_spec...  85.2 us
    unnamed x2, local copies, waits for them, and re-layouts  2.95 us

profile of v4, /device:TPU:1, one launch (start us, length us, event | category | flops | bytes accessed | tf_op | source)
XLA Modules:
  0.0 88.8 jit_solution(8678652821435064537)
XLA Ops:
  0.6 85.2 %shard_map.95 = (f32[16,8,128]{2,1,0:T(8,128)}, f32[16,8,128]{2,1,0:T(8,128)}) custom-call(bf16[1,6144,512]{2,1,0:T(8,128)(2,1)} %scores.1, s32[48,128]{1,0:T(8,128)} %bitcast.5, s32[48,128]{1,0:T(8,128)} %bitcast.6, bf16[1,48,128,128]{3,2,1,0:T(8,128)(2,1)} %covs.1, s32[8,6144]{1,0:T(8,128)} %membership_in.1, f32[48,128]{1,0:T(8,128)} %bitcast.7, ...), custom_call_target="tpu_custom_call" | custom-call | flops 500000000 | bytes 9000000 | tf_op jit(solution)/shard_map/pallas_call | solution.py:606
  85.8 1.5 %copy.12 = f32[16,8,128]{2,1,0:T(8,128)} copy(f32[16,8,128]{2,1,0:T(8,128)} %get-tuple-element.4) | data formatting | bytes 131072
  87.3 1.5 %copy.13 = f32[16,8,128]{2,1,0:T(8,128)} copy(f32[16,8,128]{2,1,0:T(8,128)} %get-tuple-element.5) | data formatting | bytes 131072
